TPU v7x, 32 devices: a whole 2x2x4 slice. The times are simulated.
32 devices in a mesh: wire: 8 (over z, y), col: 4 (over x, core).
Axes of the slice: x: 2, y: 2, z: 4, core: 2. Of those that a mesh axis runs over, the one named last changes fastest.
Arguments:
- search: float32 [24576, 384], P('wire', 'col')
- block_values: float32 [24576, 256], P('wire'), may hold values from -0.375 to 0.375
- block_cols: int32 [384, 4], P('wire'), may hold values from 0 to 383, as said below
- ritz: float32 [384, 128], replicated, may hold values from -0.3125 to 0.3125
Outputs:
- new_modes: float32 [24576, 128], P('wire', 'col')
- residual: float32 [24576, 128], P('wire', 'col')
- theta: float32 [128], P('col')
- gram_stiff: float32 [384, 384], P(None, 'col')
- gram_mass: float32 [384, 384], P(None, 'col')
Inputs may be any that keep to these rules, and one draw needn't show every extreme that they name: Block rows are in groups of 48, b in group g = b // 48. block_cols[b, 0] = b. Column 1 names a block row of group g. For even b, column 2 names a block row of group g + 1 and column 3 one of group g + 2; for odd b, groups g - 1 and g - 2; groups counted around the loop of all groups.
All inputs are finite; a program needn't handle non-finite values.
Results may differ from a plain program's by a relative error of at most 0.0003.
Values sent between devices are 32-bit elements; how exact they have to be, the bound alone decides.
A program may use at most 64 MiB of HBM per device.

v0:
```python
import jax
import jax.numpy as jnp
from jax import lax
from jax.sharding import PartitionSpec as P


def shifted(array, axis, by):
    length = lax.axis_size(axis)
    return lax.ppermute(array, axis, [(i, (i + by) % length) for i in range(length)])


def fetch_blocks(own_blocks, wanted, distance):
    asked = shifted(wanted, "wire", distance)
    served = own_blocks[asked]
    return shifted(served, "wire", -distance)


def shards(search, block_values, block_cols, ritz):
    high = lax.Precision.HIGHEST
    rows, width = search.shape
    blk = block_cols.shape[0]
    block = rows // blk
    slots = block_cols.shape[1]
    col_here = lax.axis_index("col")
    wire_here = lax.axis_index("wire")
    wire_count = lax.axis_size("wire")
    own_blocks = search.reshape(blk, block, width)
    capacity = (blk + 1) // 2
    first_row = wire_here * blk % 2
    counter = jnp.arange(capacity, dtype=jnp.int32)
    even_rows = jnp.minimum(first_row + 2 * counter, blk - 1)
    odd_rows = jnp.minimum(1 - first_row + 2 * counter, blk - 1)
    near_ahead = fetch_blocks(own_blocks, block_cols[even_rows, 2] % blk, 1)
    far_ahead = fetch_blocks(own_blocks, block_cols[even_rows, 3] % blk, 2)
    near_behind = fetch_blocks(own_blocks, block_cols[odd_rows, 2] % blk, -1)
    far_behind = fetch_blocks(own_blocks, block_cols[odd_rows, 3] % blk, -2)
    ext_blocks = jnp.concatenate(
        [own_blocks, near_ahead, far_ahead, near_behind, far_behind], axis=0
    )
    local_rows = jnp.arange(blk, dtype=jnp.int32)
    row_parity = (wire_here * blk + local_rows) % 2
    start_row = (row_parity - wire_here * blk) % 2
    position = (local_rows - start_row) // 2
    index_two = blk + jnp.where(row_parity == 0, 0, 2 * capacity) + position
    index_three = blk + jnp.where(row_parity == 0, capacity, 3 * capacity) + position
    local_index = jnp.stack(
        [block_cols[:, 0] % blk, block_cols[:, 1] % blk, index_two, index_three], axis=1
    )
    picked = ext_blocks[local_index].reshape(blk, slots * block, width)
    values = block_values.reshape(blk, block, slots * block)
    product = jnp.einsum("bik,bkc->bic", values, picked, precision=high).reshape(rows, width)
    image = 4.0 * search + product
    paired = jnp.concatenate([image, search], axis=1)
    partial_gram = jnp.einsum(
        "rk,rc->kc", lax.all_gather(search, "col", axis=1, tiled=True), paired, precision=high
    )
    mine = lax.dynamic_slice_in_dim(ritz, col_here * width, width, 0)
    modes_part = jnp.dot(search, mine, precision=high, preferred_element_type=jnp.float32)
    image_part = jnp.dot(image, mine, precision=high, preferred_element_type=jnp.float32)
    new_modes, new_image = (
        lax.psum_scatter(modes_part, "col", scatter_dimension=1, tiled=True),
        lax.psum_scatter(image_part, "col", scatter_dimension=1, tiled=True),
    )
    total_rows = jnp.float32(rows * wire_count)
    gram_total = lax.psum(partial_gram, "wire") / total_rows
    gram_stiff = gram_total[:, :width]
    gram_mass = gram_total[:, width:]
    mine_rows = lax.dynamic_slice_in_dim(ritz, col_here * width, width, 0)
    left_stiff = jnp.einsum("ab,aj->jb", gram_stiff, ritz, precision=high)
    left_mass = jnp.einsum("ab,aj->jb", gram_mass, ritz, precision=high)
    numer_terms = jnp.sum(left_stiff * mine_rows.T, axis=1)
    denom_terms = jnp.sum(left_mass * mine_rows.T, axis=1)
    sums = lax.psum_scatter(
        jnp.stack([numer_terms, denom_terms]), "col", scatter_dimension=1, tiled=True
    )
    theta = sums[0] / sums[1]
    residual = new_image - new_modes * theta[None, :]
    return (new_modes, residual, theta, gram_stiff, gram_mass)


def solution(mesh):
    placed = (P("wire", "col"), P("wire", None), P("wire", None), P())
    return jax.shard_map(
        shards,
        mesh=mesh,
        in_specs=placed,
        out_specs=(P("wire", "col"), P("wire", "col"), P("col"), P(None, "col"), P(None, "col")),
        check_vma=False,
    )
```

profile of v0, /device:TPU:9, one launch (start us, length us, event | category | flops | bytes accessed | tf_op | source)
XLA Modules:
  0.0 276.2 jit_solution(14754132788831883834)
XLA Ops:
  8.0 1.7 gather_fusion
  9.7 1.3 collective-permute-start
  11.0 1.5 gather_fusion.2
  12.5 1.3 collective-permute-start.2
  15.8 3.0 %collective-permute-start.4 = (s32[24]{0:T(128)S(1)}, s32[24]{0:T(128)S(1)}, u32[]{:S(2)}, u32[]{:S(2)}) collective-permute-start(s32[24]{0:T(128)S(1)} %and_select_fusion.6), channel_id=1, source_target_pairs={{0,28},{4,0},{8,4},{12,8},{16,12},{20,16},{24,20},{28,24},{1,29},{... | collective-permute-start | bytes 296 | tf_op jit(solution)/shard_map/ppermute | solution.py:9
  18.8 3.0 %copy.14 = f32[3072,96]{1,0:T(8,128)} copy(f32[3072,96]{0,1:T(8,128)} %param.4) | data formatting | bytes 2359296 | tf_op args[0]
  21.9 2.9 %gather_fusion.1 = f32[24,64,96]{2,1,0:T(8,128)} fusion(f32[48,64,96]{2,1,0:T(8,128)} %bitcast.44, s32[1024]{0:T(1024)S(1)} %pad_clamp_fusion.4), kind=kCustom, calls=%fused_computation.1 | custom fusion | bytes 1179744 | tf_op jit(solution)/shard_map/gather | solution.py:14
  25.2 2.9 %gather_fusion.3 = f32[24,64,96]{2,1,0:T(8,128)} fusion(f32[48,64,96]{2,1,0:T(8,128)} %bitcast.45, s32[1024]{0:T(1024)S(1)} %pad_clamp_fusion.3), kind=kCustom, calls=%fused_computation.3 | custom fusion | bytes 1179744 | tf_op jit(solution)/shard_map/gather | solution.py:14
  28.2 1.5 collective-permute-start.3
  29.7 2.9 %gather_fusion.5 = f32[24,64,96]{2,1,0:T(8,128)} fusion(f32[48,64,96]{2,1,0:T(8,128)} %bitcast.46, s32[1024]{0:T(1024)S(1)} %get-tuple-element.16), kind=kCustom, calls=%fused_computation.5 | custom fusion | bytes 1179744 | tf_op jit(solution)/shard_map/gather | solution.py:14
  32.8 2.9 %gather_fusion.7 = f32[24,64,96]{2,1,0:T(8,128)} fusion(f32[48,64,96]{2,1,0:T(8,128)} %bitcast.47, s32[1024]{0:T(1024)S(1)} %get-tuple-element.15), kind=kCustom, calls=%fused_computation.7 | custom fusion | bytes 1179744 | tf_op jit(solution)/shard_map/gather | solution.py:14
  36.7 2.8 constant_dynamic-update-slice_fusion.4
  39.5 2.8 %collective-permute-done.1 = f32[24,64,96]{2,1,0:T(8,128)} collective-permute-done((f32[24,64,96]{2,1,0:T(8,128)}, f32[24,64,96]{2,1,0:T(8,128)}, u32[]{:S(2)}, u32[]{:S(2)}) %collective-permute-start.1) | collective-permute-done | bytes 589856 | tf_op jit(solution)/shard_map/ppermute | solution.py:9
  42.3 2.2 constant_dynamic-update-slice_fusion.3
  44.4 13.2 %collective-permute-done.3 = f32[24,64,96]{2,1,0:T(8,128)} collective-permute-done((f32[24,64,96]{2,1,0:T(8,128)}, f32[24,64,96]{2,1,0:T(8,128)}, u32[]{:S(2)}, u32[]{:S(2)}) %collective-permute-start.3) | collective-permute-done | bytes 589856 | tf_op jit(solution)/shard_map/ppermute | solution.py:9
  57.7 2.1 constant_dynamic-update-slice_fusion.2
  59.8 3.9 %collective-permute-done.5 = f32[24,64,96]{2,1,0:T(8,128)} collective-permute-done((f32[24,64,96]{2,1,0:T(8,128)}, f32[24,64,96]{2,1,0:T(8,128)}, u32[]{:S(2)}, u32[]{:S(2)}) %collective-permute-start.5) | collective-permute-done | bytes 589856 | tf_op jit(solution)/shard_map/ppermute | solution.py:9
  63.7 2.1 constant_dynamic-update-slice_fusion.1
  65.8 11.9 %collective-permute-done.7 = f32[24,64,96]{2,1,0:T(8,128)S(1)} collective-permute-done((f32[24,64,96]{2,1,0:T(8,128)}, f32[24,64,96]{2,1,0:T(8,128)S(1)}, u32[]{:S(2)}, u32[]{:S(2)}) %collective-permute-start.7) | collective-permute-done | bytes 589856 | tf_op jit(solution)/shard_map/ppermute | solution.py:9
  78.7 6.0 %gather_fusion.8 = f32[192,64,96]{2,1,0:T(8,128)} fusion(f32[144,64,96]{2,1,0:T(8,128)} %constant_dynamic-update-slice_fusion, s32[1024]{0:T(1024)S(1)} %pad_clamp_fusion), kind=kCustom, calls=%fused_computation.8 | custom fusion | bytes 9437952 | tf_op jit(solution)/shard_map/gather | solution.py:49
  84.7 7.2 %fusion.32 = f32[48,96,64]{1,2,0:T(8,128)} fusion(f32[48,256,96]{2,1,0:T(8,128)} %bitcast.49, f32[48,64,256]{2,1,0:T(8,128)S(1)} %bitcast.43), kind=kOutput, calls=%fused_computation.87 | convolution fusion | flops 905969664 | bytes 9043968 | tf_op jit(solution)/shard_map/bik,bkc->bic/dot_general | solution.py:51
  91.9 2.9 %copy.17 = f32[3072,96]{0,1:T(8,128)} copy(f32[3072,96]{1,0:T(8,128)} %bitcast.50) | data formatting | bytes 2359296 | tf_op jit(solution)/shard_map/reshape | solution.py:51
  94.8 2.8 %multiply_add_fusion = f32[3072,96]{0,1:T(8,128)} fusion(f32[3072,96]{0,1:T(8,128)} %copy.17, f32[3072,96]{0,1:T(8,128)} %param.4), kind=kLoop, calls=%fused_computation.14 | loop fusion | flops 589824 | bytes 3538944 | tf_op jit(solution)/shard_map/add | solution.py:52
  97.6 8.7 %fusion.4 = f32[384,192]{0,1:T(8,128)} fusion(f32[3072,384]{0,1:T(8,128)} %all-gather.2.cloned.1.call-done, f32[3072,96]{0,1:T(8,128)} %param.4, f32[3072,96]{0,1:T(8,128)} %multiply_add_fusion), kind=kOutput, calls=%fused_computation.15 | convolution fusion | flops 2718498816 | bytes 7372800 | tf_op jit(solution)/shard_map/rk,rc->kc/dot_general | solution.py:54
  106.5 74.7 %all-reduce.6.cloned.1.call-done = f32[384,192]{0,1:T(8,128)} async-done(((f32[384,192]{0,1:T(8,128)}), f32[384,192]{0,1:T(8,128)}) %all-reduce.6.cloned.1.call-update) | async-done | bytes 294928 | tf_op jit(solution)/shard_map/psum | solution.py:65
  181.2 1.0 broadcast_multiply_fusion
  184.0 3.9 %convolution_bitcast_fusion = f32[3072,128]{0,1:T(8,128)} fusion(f32[3072,96]{0,1:T(8,128)} %param.4, f32[384,128]{1,0:T(8,128)S(1)} %copy-done.2, s32[]{:T(128)S(6)} %select_n.248), kind=kOutput, calls=%fused_computation.9 | convolution fusion | flops 452984832 | bytes 2801668 | tf_op jit(solution)/shard_map/dot_general | solution.py:58
  188.0 3.9 %fusion.9 = f32[3072,128]{0,1:T(8,128)} fusion(f32[3072,96]{0,1:T(8,128)} %multiply_add_fusion, f32[384,128]{1,0:T(8,128)S(1)} %copy-done.2, s32[]{:T(128)S(6)} %select_n.248), kind=kOutput, calls=%fused_computation.22 | convolution fusion | flops 452984832 | bytes 2801668 | tf_op jit(solution)/shard_map/dot_general | solution.py:59
  191.9 13.4 %reduce-scatter.10.cloned.1.call-done = f32[32,2]{1,0:T(8,128)} async-done(((f32[128,2]{1,0:T(8,128)}), f32[32,2]{1,0:T(8,128)}) %reduce-scatter.10.cloned.1.call-update) | async-done | bytes 272
  206.3 30.6 %reduce-scatter.6.cloned.1.call-done = f32[3072,32]{0,1:T(8,128)} async-done(((f32[3072,128]{0,1:T(8,128)}), f32[3072,32]{0,1:T(8,128)}) %reduce-scatter.6.cloned.1.call-update) | async-done | bytes 393232 | tf_op jit(solution)/shard_map/reduce_scatter | solution.py:61
  236.9 30.7 %reduce-scatter.8.cloned.1.call-done = f32[3072,32]{0,1:T(8,128)} async-done(((f32[3072,128]{0,1:T(8,128)}), f32[3072,32]{0,1:T(8,128)}) %reduce-scatter.8.cloned.1.call-update) | async-done | bytes 393232 | tf_op jit(solution)/shard_map/reduce_scatter | solution.py:62
  267.7 2.0 multiply_subtract_fusion
  (63 shorter events, 8.6 us)
Async XLA Ops:
  7.2 77.5 %copy-start = (f32[3072,256]{1,0:T(8,128)S(1)}, f32[3072,256]{1,0:T(8,128)}, u32[]{:S(2)}) copy-start(f32[3072,256]{1,0:T(8,128)} %param.5) | copy-start | bytes 9437188
  7.2 6.7 %copy-start.1 = (s32[48,4]{0,1:T(4,128)S(1)}, s32[48,4]{0,1:T(4,128)}, u32[]{:S(2)}) copy-start(s32[48,4]{0,1:T(4,128)} %param.6) | copy-start | bytes 2308
  7.2 90.4 %all-gather.2.cloned.1.call-start = ((), (), s32[]{:S(2)}) async-start(), calls=%async_computation.5 | async-start | bytes 5898240 | tf_op jit(solution)/shard_map/all_gather | solution.py:55
  7.9 173.3 %all-reduce.6.cloned.1.call-start = ((), (), s32[]{:S(2)}) async-start(), calls=%async_computation.6 | async-start | bytes 589824 | tf_op jit(solution)/shard_map/psum | solution.py:65
  9.7 12.2 %collective-permute-start = (s32[24]{0:T(128)S(1)}, s32[24]{0:T(128)S(1)}, u32[]{:S(2)}, u32[]{:S(2)}) collective-permute-start(s32[24]{0:T(128)S(1)} %and_select_fusion.8), channel_id=1, source_target_pairs={{0,4},{4,8},{8,12},{12,16},{16,20},{20,24},{24,28},{28,0},{1,5},{5... | collective-permute-start | bytes 296 | tf_op jit(solution)/shard_map/ppermute | solution.py:9
  12.5 12.7 %collective-permute-start.2 = (s32[24]{0:T(128)S(1)}, s32[24]{0:T(128)S(1)}, u32[]{:S(2)}, u32[]{:S(2)}) collective-permute-start(s32[24]{0:T(128)S(1)} %and_select_fusion.7), channel_id=1, source_target_pairs={{0,8},{4,12},{8,16},{12,20},{16,24},{20,28},{24,0},{28,4},{1,9},{5... | collective-permute-start | bytes 296 | tf_op jit(solution)/shard_map/ppermute | solution.py:9
  14.7 14.9 %collective-permute-start.6 = (s32[24]{0:T(128)S(1)}, s32[24]{0:T(128)S(1)}, u32[]{:S(2)}, u32[]{:S(2)}) collective-permute-start(s32[24]{0:T(128)S(1)} %and_select_fusion.5), channel_id=1, source_target_pairs={{0,24},{4,28},{8,0},{12,4},{16,8},{20,12},{24,16},{28,20},{1,25},{... | collective-permute-start | bytes 296 | tf_op jit(solution)/shard_map/ppermute | solution.py:9
  15.8 13.8 %collective-permute-start.4 = (s32[24]{0:T(128)S(1)}, s32[24]{0:T(128)S(1)}, u32[]{:S(2)}, u32[]{:S(2)}) collective-permute-start(s32[24]{0:T(128)S(1)} %and_select_fusion.6), channel_id=1, source_target_pairs={{0,28},{4,0},{8,4},{12,8},{16,12},{20,16},{24,20},{28,24},{1,29},{... | collective-permute-start | bytes 296 | tf_op jit(solution)/shard_map/ppermute | solution.py:9
  24.8 17.5 %collective-permute-start.1 = (f32[24,64,96]{2,1,0:T(8,128)}, f32[24,64,96]{2,1,0:T(8,128)}, u32[]{:S(2)}, u32[]{:S(2)}) collective-permute-start(f32[24,64,96]{2,1,0:T(8,128)} %gather_fusion.1), channel_id=1, source_target_pairs={{0,28},{4,0},{8,4},{12,8},{16,12},{20,16},{24,20},{28,24},{1,29},{... | collective-permute-start | bytes 1769480 | tf_op jit(solution)/shard_map/ppermute | solution.py:9
  28.2 29.5 %collective-permute-start.3 = (f32[24,64,96]{2,1,0:T(8,128)}, f32[24,64,96]{2,1,0:T(8,128)}, u32[]{:S(2)}, u32[]{:S(2)}) collective-permute-start(f32[24,64,96]{2,1,0:T(8,128)} %gather_fusion.3), channel_id=1, source_target_pairs={{0,24},{4,28},{8,0},{12,4},{16,8},{20,12},{24,16},{28,20},{1,25},{... | collective-permute-start | bytes 1769480 | tf_op jit(solution)/shard_map/ppermute | solution.py:9
  32.6 31.1 %collective-permute-start.5 = (f32[24,64,96]{2,1,0:T(8,128)}, f32[24,64,96]{2,1,0:T(8,128)}, u32[]{:S(2)}, u32[]{:S(2)}) collective-permute-start(f32[24,64,96]{2,1,0:T(8,128)} %gather_fusion.5), channel_id=1, source_target_pairs={{0,4},{4,8},{8,12},{12,16},{16,20},{20,24},{24,28},{28,0},{1,5},{5... | collective-permute-start | bytes 1769480 | tf_op jit(solution)/shard_map/ppermute | solution.py:9
  35.7 42.0 %collective-permute-start.7 = (f32[24,64,96]{2,1,0:T(8,128)}, f32[24,64,96]{2,1,0:T(8,128)S(1)}, u32[]{:S(2)}, u32[]{:S(2)}) collective-permute-start(f32[24,64,96]{2,1,0:T(8,128)} %gather_fusion.7), channel_id=1, source_target_pairs={{0,8},{4,12},{8,16},{12,20},{16,24},{20,28},{24,0},{28,4},{1,9},{5... | collective-permute-start | bytes 1769480 | tf_op jit(solution)/shard_map/ppermute | solution.py:9
  97.6 84.7 %copy-start.2 = (f32[384,128]{1,0:T(8,128)S(1)}, f32[384,128]{1,0:T(8,128)}, u32[]{:S(2)}) copy-start(f32[384,128]{1,0:T(8,128)} %param.7) | copy-start | bytes 589828
  106.3 99.0 %reduce-scatter.10.cloned.1.call-start = ((), (), s32[]{:S(2)}) async-start(), calls=%async_computation.7 | async-start | bytes 81920
  182.2 0.7 copy-start.4
  182.3 5.7 %copy-start.3 = (f32[384,96]{0,1:T(8,128)}, f32[384,96]{0,1:T(8,128)S(1)}, u32[]{:S(2)}) copy-start(f32[384,96]{0,1:T(8,128)S(1)} %get-tuple-element.5) | copy-start | bytes 442372
  184.0 52.9 %reduce-scatter.6.cloned.1.call-start = ((), (), s32[]{:S(2)}) async-start(), calls=%async_computation.3 | async-start | bytes 1966080 | tf_op jit(solution)/shard_map/reduce_scatter | solution.py:61
  188.0 79.7 %reduce-scatter.8.cloned.1.call-start = ((), (), s32[]{:S(2)}) async-start(), calls=%async_computation.4 | async-start | bytes 1966080 | tf_op jit(solution)/shard_map/reduce_scatter | solution.py:62
  206.3 63.3 %copy-start.5 = (f32[32]{0:T(128)}, f32[32]{0:T(128)S(1)}, u32[]{:S(2)}) copy-start(f32[32]{0:T(128)S(1)} %divide_bitcast_fusion) | copy-start | bytes 388
Sparse Core Ops, SparseCore 0:
  9.6 39.0 all-gather.1
  106.4 74.7 all-reduce.5
  184.4 20.8 reduce-scatter.9
  208.2 28.6 reduce-scatter.5
  239.5 28.1 reduce-scatter.7
where the time goes:
time: 278 us; the launch traced here: 276 us
  waiting for transfers between devices  182 us (65%)
  local copies, waits for them, and re-layouts  40.8 us (15%)
  matrix products  24.2 us (9%)
  between operations  13.9 us (5%)
  starting transfers between devices  9.13 us (3%)
  other arithmetic  5.93 us (2%)
    psum x1, waiting for transfers between devices, shards(): gram_total = lax.psum(partial_gram, 'wire') / total_rows  74.7 us
    ppermute x8, waiting for transfers between devices, shifted(): lax.ppermute(array, axis, [(i, (i + by) % length) for i in range(length)])  31.9 us
    reduce_scatter x1, waiting for transfers between devices, shards(): lax.psum_scatter(image_part, 'col', scatter_dimension=1, tiled=True)  30.7 us
    reduce_scatter x1, waiting for transfers between devices, shards(): lax.psum_scatter(modes_part, 'col', scatter_dimension=1, tiled=True)  30.6 us
    unnamed x6, waiting for transfers between devices  14.1 us
    unnamed x20, local copies, waits for them, and re-layouts  13.4 us
    gather x4, local copies, waits for them, and re-layouts, fetch_blocks(): served = own_blocks[asked]  11.6 us
    ppermute x8, starting transfers between devices, shifted(): lax.ppermute(array, axis, [(i, (i + by) % length) for i in range(length)])  8.75 us
  transfers between devices with their start and end apart: 13, of which 8 were waited for; matrix products, arithmetic and copies ran while one was open for 21% of the time, Pallas kernels for 0%

commit v1 on v0

v1 whole, which is shorter than its diff:
```python
import functools

import jax
import jax.numpy as jnp
from jax import lax
from jax.experimental import pallas as pl
from jax.experimental.pallas import tpu as pltpu
from jax.sharding import PartitionSpec as P

MESH = pl.DeviceIdType.MESH
DISTANCES = (1, 2, -1, -2)
NN = (((1,), (0,)), ((), ()))
NT = (((1,), (1,)), ((), ()))


def split(x):
    high = x.astype(jnp.bfloat16)
    return high, (x - high.astype(jnp.float32)).astype(jnp.bfloat16)


def product(a, b, dims=NN):
    mul = functools.partial(lax.dot_general, dimension_numbers=dims, preferred_element_type=jnp.float32)
    return mul(a[0], b[0]) + (mul(a[0], b[1]) + mul(a[1], b[0]))


def remote(src, dst, send, recv, device):
    return pltpu.make_async_remote_copy(
        src_ref=src, dst_ref=dst, send_sem=send, recv_sem=recv, device_id=device, device_id_type=MESH
    )


def kernel(
    nw, nc, parts, total_rows,
    asked, near, search, values, rcols, rmine,
    modes_out, resid_out, theta_out, grams_out,
    stage, halo, others, st_hi, st_lo, image, part, got, gram, gram_got, gram_full, terms, terms_got,
    halo_send, halo_recv, all_send, all_recv, sum_send, sum_recv,
    red_send, red_recv, bc_send, bc_recv, th_send, th_recv,
):
    blk, block, width = search.shape
    half = blk // 2
    wide = gram.shape[1]
    mc = rcols.shape[0]
    rows = blk * block
    span = rows // parts
    bspan = blk // parts
    hspan = half // parts
    chunk = gram_got.shape[2]
    owners = wide // chunk
    w = lax.axis_index("wire")
    c = lax.axis_index("col")

    def on_wire(k):
        return lax.rem(w + k + nw, nw)

    def on_col(k):
        return lax.rem(c + k + nc, nc)

    barrier = pltpu.get_barrier_semaphore()

    @pl.loop(1, nw)
    def _(k):
        pl.semaphore_signal(barrier, inc=1, device_id={"wire": on_wire(k)}, device_id_type=MESH)

    for k in range(1, nc):
        pl.semaphore_signal(barrier, inc=1, device_id={"col": on_col(k)}, device_id_type=MESH)

    def fetch(t):
        @pl.loop(t * hspan, (t + 1) * hspan)
        def _(j):
            for d in range(4):
                stage[d, j] = search[asked[d, j]]

    def halo_copy(d, t):
        js = pl.ds(t * hspan, hspan)
        return remote(
            stage.at[d, js], halo.at[d, js], halo_send.at[d, t], halo_recv.at[d, t],
            {"wire": on_wire(-DISTANCES[d])},
        )

    def all_copy(k):
        return remote(search, others.at[c], all_send.at[k - 1], all_recv.at[k - 1], {"col": on_col(k)})

    def all_arrival(k):
        return remote(
            search, others.at[on_col(-k)], all_send.at[k - 1], all_recv.at[k - 1], {"col": on_col(k)}
        )

    def sum_copy(k, t):
        ls = pl.ds(t * span, span)
        return remote(
            part.at[on_col(k), :, ls], got.at[k - 1, :, ls],
            sum_send.at[k - 1, t], sum_recv.at[k - 1, t], {"col": on_col(k)},
        )

    def red_copy(g, k):
        p = on_wire(k)
        first = pl.multiple_of(lax.rem(p, owners) * chunk, 8)
        return remote(
            gram.at[g, pl.ds(first, chunk)], gram_got.at[g, k],
            red_send.at[g, k], red_recv.at[g, k], {"wire": p},
        )

    def start_red(g):
        @pl.loop(1, nw)
        def _(k):
            if owners == nw:
                red_copy(g, k).start()
            else:
                @pl.when(on_wire(k) < owners)
                def _():
                    red_copy(g, k).start()

    def bc_copy(k, origin):
        first = pl.multiple_of(lax.rem(origin, owners) * chunk, 8)
        view = gram_full.at[:, pl.ds(first, chunk)]
        return remote(view, view, bc_send.at[k], bc_recv.at[k], {"wire": on_wire(k)})

    def th_copy(k):
        return remote(terms, terms_got.at[k], th_send.at[k], th_recv.at[k], {"wire": on_wire(k)})

    fetch(0)
    others[c] = search[...]
    pl.semaphore_wait(barrier, nw + nc - 2)
    for t in range(parts):
        if t > 0:
            fetch(t)
        for d in (3, 1, 0, 2):
            halo_copy(d, t).start()
    for k in range(1, nc):
        all_copy(k).start()

    def turn(q):
        @pl.loop(0, parts)
        def _(t):
            at = others[q, pl.ds(t * bspan, bspan)].reshape(span, width).T
            high, low = split(at)
            ls = pl.ds(pl.multiple_of(t * span, 128), span)
            rs = pl.ds(pl.multiple_of(q * width, 16), width)
            st_hi[rs, ls] = high
            st_lo[rs, ls] = low

    turn(c)
    for k in range(1, nc):
        all_arrival(k).wait_recv()
        turn(on_col(-k))

    rc = split(rcols[...])
    gram[...] = jnp.zeros_like(gram)

    @pl.loop(0, parts)
    def _(t):
        ls = pl.ds(pl.multiple_of(t * span, 128), span)
        here = (st_hi[:, ls], st_lo[:, ls])
        own = split(search[pl.ds(t * bspan, bspan)].reshape(span, width))
        gram[1] += product(here, own)
        modes_out[:, ls] = product(rc, here)

    start_red(1)

    rm = split(rmine[...])
    for t in range(parts):
        for d in range(4):
            halo_copy(d, t).wait_recv()

        @pl.loop(t * hspan, (t + 1) * hspan)
        def _(j):
            for odd in range(2):
                i = 2 * j + odd
                picked = jnp.concatenate(
                    [search[i], search[near[i]], halo[2 * odd, j], halo[2 * odd + 1, j]], axis=0
                )
                image[i] = 4.0 * search[i] + product(split(values[i]), split(picked))

        img = split(image[t * bspan:(t + 1) * bspan].reshape(span, width))
        turned = product(rm, img, NT)
        for q in range(nc):
            part[q, :, t * span:(t + 1) * span] = turned[q * mc:(q + 1) * mc]
        for k in range(1, nc):
            sum_copy(k, t).start()
        here = (st_hi[:, t * span:(t + 1) * span], st_lo[:, t * span:(t + 1) * span])
        gram[0] += product(here, img)

    start_red(0)

    numer = jnp.zeros((mc, 1), jnp.float32)
    denom = jnp.zeros((mc, 1), jnp.float32)
    for t in range(parts):
        ls = slice(t * span, (t + 1) * span)
        for k in range(1, nc):
            sum_copy(k, t).wait_recv()
        mine = part[c, :, ls]
        for k in range(1, nc):
            mine = mine + got[k - 1, :, ls]
        resid_out[:, ls] = mine
        modes = modes_out[:, ls]
        numer = numer + jnp.sum(modes * mine, axis=1, keepdims=True)
        denom = denom + jnp.sum(modes * modes, axis=1, keepdims=True)
    lane = lax.broadcasted_iota(jnp.int32, terms.shape, 1)
    terms[...] = jnp.where(lane < 64, numer, denom)

    @pl.loop(1, nw)
    def _(k):
        th_copy(k).start()

    def own_chunk():
        first = pl.multiple_of(lax.rem(w, owners) * chunk, 8)
        for g in range(2):
            gram_got[g, 0] = gram[g, pl.ds(first, chunk)]

            @pl.loop(1, nw)
            def _(k):
                red_copy(g, k).wait_recv()
                gram_got[g, 0] += gram_got[g, k]

            gram_full[g, pl.ds(first, chunk)] = gram_got[g, 0] * (1.0 / total_rows)

        @pl.loop(1, nw)
        def _(k):
            bc_copy(k, w).start()

    if owners == nw:
        own_chunk()
    else:
        pl.when(w < owners)(own_chunk)

    terms_got[0] = terms[...]

    @pl.loop(1, nw)
    def _(k):
        th_copy(k).wait_recv()
        terms_got[0] += terms_got[k]

    sums = terms_got[0]
    theta = sums[:, 0:1] / sums[:, 64:65]
    theta_out[...] = jnp.broadcast_to(theta, theta_out.shape)
    resid_out[...] = resid_out[...] - modes_out[...] * theta

    @pl.loop(1, nw)
    def _(k):
        th_copy(k).wait_send()
        if owners == nw:
            bc_copy(k, on_wire(-k)).wait_recv()
            bc_copy(k, w).wait_send()
            red_copy(0, k).wait_send()
            red_copy(1, k).wait_send()
        else:
            @pl.when(on_wire(-k) < owners)
            def _():
                bc_copy(k, on_wire(-k)).wait_recv()

            @pl.when(w < owners)
            def _():
                bc_copy(k, w).wait_send()

            @pl.when(on_wire(k) < owners)
            def _():
                red_copy(0, k).wait_send()
                red_copy(1, k).wait_send()

    grams_out[...] = gram_full[...]
    for t in range(parts):
        for d in range(4):
            halo_copy(d, t).wait_send()
        for k in range(1, nc):
            sum_copy(k, t).wait_send()
    for k in range(1, nc):
        all_copy(k).wait_send()


def shards(search, block_values, block_cols, ritz):
    rows, width = search.shape
    blk, slots = block_cols.shape
    assert blk % 2 == 0 and slots == 4
    block = rows // blk
    half = blk // 2
    wide, modes = ritz.shape
    nw, nc = lax.axis_size("wire"), lax.axis_size("col")
    mc = modes // nc
    c = lax.axis_index("col")
    parts = next(n for n in (3, 2, 1) if half % n == 0 and (rows // n) % 128 == 0)
    chunk = max(8, -(-wide // nw) // 8 * 8)
    assert wide % chunk == 0 and wide // chunk <= nw
    owners = wide // chunk
    local = block_cols % blk
    asked = []
    for distance, wanted in zip(
        DISTANCES, (local[0::2, 2], local[0::2, 3], local[1::2, 2], local[1::2, 3])
    ):
        asked.append(lax.ppermute(wanted, "wire", [(i, (i + distance) % nw) for i in range(nw)]))
    asked = jnp.stack(asked)
    rcols = lax.dynamic_slice_in_dim(ritz, c * mc, mc, 1).T
    rmine = lax.dynamic_slice_in_dim(ritz, c * width, width, 0).T
    f32 = jnp.float32
    vmem = pl.BlockSpec(memory_space=pltpu.VMEM)
    smem = pl.BlockSpec(memory_space=pltpu.SMEM)
    dma = pltpu.SemaphoreType.DMA
    modes_t, resid_t, theta, grams = pl.pallas_call(
        functools.partial(kernel, nw, nc, parts, float(rows * nw)),
        out_shape=(
            jax.ShapeDtypeStruct((mc, rows), f32),
            jax.ShapeDtypeStruct((mc, rows), f32),
            jax.ShapeDtypeStruct((mc, 128), f32),
            jax.ShapeDtypeStruct((2, wide, width), f32),
        ),
        in_specs=[smem, smem, vmem, vmem, vmem, vmem],
        out_specs=(vmem,) * 4,
        scratch_shapes=[
            pltpu.VMEM((4, half, block, width), f32),
            pltpu.VMEM((4, half, block, width), f32),
            pltpu.VMEM((nc, blk, block, width), f32),
            pltpu.VMEM((wide, rows), jnp.bfloat16),
            pltpu.VMEM((wide, rows), jnp.bfloat16),
            pltpu.VMEM((blk, block, width), f32),
            pltpu.VMEM((nc, mc, rows), f32),
            pltpu.VMEM((nc - 1, mc, rows), f32),
            pltpu.VMEM((2, wide, width), f32),
            pltpu.VMEM((2, nw, chunk, width), f32),
            pltpu.VMEM((2, wide, width), f32),
            pltpu.VMEM((mc, 128), f32),
            pltpu.VMEM((nw, mc, 128), f32),
            dma((4, parts)), dma((4, parts)),
            dma((nc - 1,)), dma((nc - 1,)),
            dma((nc - 1, parts)), dma((nc - 1, parts)),
            dma((2, nw)), dma((2, nw)),
            dma((nw,)), dma((nw,)),
            dma((nw,)), dma((nw,)),
        ],
        compiler_params=pltpu.CompilerParams(
            collective_id=0, has_side_effects=True, vmem_limit_bytes=56 * 1024 * 1024
        ),
        name="step",
    )(asked, local[:, 1], search.reshape(blk, block, width),
      block_values.reshape(blk, block, slots * block), rcols, rmine)
    return modes_t.T, resid_t.T, theta[:, 0], grams[0], grams[1]


def solution(mesh):
    placed = (P("wire", "col"), P("wire", None), P("wire", None), P())
    return jax.shard_map(
        shards,
        mesh=mesh,
        in_specs=placed,
        out_specs=(P("wire", "col"), P("wire", "col"), P("col"), P(None, "col"), P(None, "col")),
        check_vma=False,
    )
```

time: 278 us -> 124 us (0.45)
  waiting for transfers between devices: 182 us -> 0.01 us
  Pallas kernels: 0 us -> 105 us
  local copies, waits for them, and re-layouts: 40.8 us -> 11 us
  matrix products: 24.2 us -> 0 us
  between operations: 13.9 us -> 0.7 us
  other arithmetic: 5.93 us -> 1.32 us
  starting transfers between devices: 9.13 us -> 5.83 us
    pallas_call x0 -> x1, Pallas kernels: none -> 105 us  [shards(): pl.pallas_call(functools.partial(kernel, nw, nc, parts, float(rows * nw))...]
    psum x1 -> x0, waiting for transfers between devices: 74.7 us -> none  [shards(): gram_total = lax.psum(partial_gram, 'wire') / total_rows]
    reduce_scatter x2 -> x0, waiting for transfers between devices: 61.4 us -> none  [the longest x1 30.7 us: shards(): lax.psum_scatter(image_part, 'col', scatter_dimension=1, tiled=True)]
    ppermute x8 -> x4, waiting for transfers between devices: 31.9 us -> 0.01 us  [shards(): lax.ppermute(wanted, 'wire', [(i, (i + distance) % nw) for i in range(nw)])]
    dot_general x6 -> x0, matrix products: 24.2 us -> none  [the longest x1 8.66 us: shards(): jnp.einsum('rk,rc->kc', lax.all_gather(search, 'col', axis=1, tiled=True)...]
    gather x9 -> x0, local copies, waits for them, and re-layouts: 22.5 us -> none  [the longest x4 11.6 us: fetch_blocks(): served = own_blocks[asked]]
    unnamed x6 -> x0, waiting for transfers between devices: 14.1 us -> none
    unnamed x20 -> x13, local copies, waits for them, and re-layouts: 13.4 us -> 7.44 us
  transfers between devices with their start and end apart: 13 -> 4, of which waited for: 8 -> 0; matrix products, arithmetic and copies ran while one was open for 21% -> 4% of each run, Pallas kernels for 0% -> 0%
where the time goes in v1:
time: 124 us
  Pallas kernels  105 us (85%)
  local copies, waits for them, and re-layouts  11 us (9%)
  starting transfers between devices  5.83 us (5%)
  other arithmetic  1.32 us (1%)
    pallas_call x1, Pallas kernels, shards(): pl.pallas_call(functools.partial(kernel, nw, nc, parts, float(rows * nw))...  105 us
    unnamed x13, local copies, waits for them, and re-layouts  7.44 us
    ppermute x4, starting transfers between devices, shards(): lax.ppermute(wanted, 'wire', [(i, (i + distance) % nw) for i in range(nw)])  5.83 us
  transfers between devices with their start and end apart: 4, of which 0 were waited for; matrix products, arithmetic and copies ran while one was open for 4% of the time, Pallas kernels for 0%

profile of v1, /device:TPU:9, one launch (start us, length us, event | category | flops | bytes accessed | tf_op | source)
XLA Modules:
  0.0 123.6 jit_solution(10512547604328633751)
XLA Ops:
  0.6 0.0 copy-start
  0.6 0.7 add_select_fusion
  1.4 0.1 slice.25
  1.5 1.3 %collective-permute-start.1 = (s32[24]{0:T(128)S(1)}, s32[24]{0:T(128)S(1)}, u32[]{:S(2)}, u32[]{:S(2)}) collective-permute-start(s32[24]{0:T(128)S(1)} %bitcast.30), channel_id=1, source_target_pairs={{0,8},{4,12},{8,16},{12,20},{16,24},{20,28},{24,0},{28,4},{1,9},{5... | collective-permute-start | bytes 296 | tf_op jit(solution)/shard_map/ppermute | solution.py:290
  2.8 0.1 slice.24
  2.9 1.3 %collective-permute-start = (s32[24]{0:T(128)S(1)}, s32[24]{0:T(128)S(1)}, u32[]{:S(2)}, u32[]{:S(2)}) collective-permute-start(s32[24]{0:T(128)S(1)} %bitcast.31), channel_id=1, source_target_pairs={{0,4},{4,8},{8,12},{12,16},{16,20},{20,24},{24,28},{28,0},{1,5},{5... | collective-permute-start | bytes 296 | tf_op jit(solution)/shard_map/ppermute | solution.py:290
  4.2 0.1 slice.26
  4.3 1.2 collective-permute-start.2
  5.5 0.1 slice.27
  5.6 2.0 %collective-permute-start.3 = (s32[24]{0:T(128)S(1)}, s32[24]{0:T(128)S(1)}, u32[]{:S(2)}, u32[]{:S(2)}) collective-permute-start(s32[24]{0:T(128)S(1)} %bitcast.33), channel_id=1, source_target_pairs={{0,24},{4,28},{8,0},{12,4},{16,8},{20,12},{24,16},{28,20},{1,25},{... | collective-permute-start | bytes 296 | tf_op jit(solution)/shard_map/ppermute | solution.py:290
  7.7 0.5 slice_bitcast_fusion.2.near
  8.2 0.0 copy-done
  8.2 0.7 copy.20
  8.9 0.1 constant_dynamic-slice_fusion.1
  9.0 0.7 copy.19
  9.8 2.9 %copy.14 = f32[3072,96]{1,0:T(8,128)} copy(f32[3072,96]{0,1:T(8,128)} %param.4) | data formatting | bytes 2359296 | tf_op args[0]
  12.7 0.0 collective-permute-done.1
  12.7 0.0 collective-permute-done
  12.7 0.0 collective-permute-done.2
  12.7 0.0 collective-permute-done.3
  12.7 0.6 pad_add_fusion.asked
  13.3 104.8 %step.1 = (f32[32,3072]{1,0:T(8,128)}, f32[32,3072]{1,0:T(8,128)}, f32[32,128]{1,0:T(8,128)}, f32[2,384,96]{2,1,0:T(8,128)}) custom-call(s32[4,24]{1,0:T(4,128)} %pad_add_fusion.asked, s32[48]{0:T(128)} %slice_bitcast_fusion.2.near, f32[48,64,96]{2,1,0:T(8,128)} %bitcast.20, f32[48,64,256]{2,1,0:T(8,128)} %bitcast.21, f32[32,384]{1,0:T(8,128)} %bitcast.25, ...), custom_call_target="tpu_custom_call" | custom-call | tf_op jit(solution)/shard_map/step/pallas_call | solution.py:298
  118.1 0.0 copy-start.2
  118.1 0.0 copy-start.1
  118.1 1.4 %slice_reduce_fusion = f32[32]{0:T(128)} fusion(f32[32,128]{1,0:T(8,128)} %get-tuple-element.11), kind=kLoop, calls=%fused_computation.2 | loop fusion | bytes 256 | tf_op jit(solution)/shard_map/slice | solution.py:335
  119.5 1.0 slice_bitcast_fusion
  120.6 0.8 copy.18
  121.3 0.8 copy.17
  122.1 0.0 copy-done.2
  122.1 0.7 copy.23
  122.9 0.0 copy-done.1
  122.9 0.7 copy.24
  (1 shorter events, 0.0 us)
Async XLA Ops:
  0.6 7.5 %copy-start = (f32[384,128]{1,0:T(8,128)S(1)}, f32[384,128]{1,0:T(8,128)}, u32[]{:S(2)}) copy-start(f32[384,128]{1,0:T(8,128)} %param.7) | copy-start | bytes 589828
  1.5 11.2 %collective-permute-start.1 = (s32[24]{0:T(128)S(1)}, s32[24]{0:T(128)S(1)}, u32[]{:S(2)}, u32[]{:S(2)}) collective-permute-start(s32[24]{0:T(128)S(1)} %bitcast.30), channel_id=1, source_target_pairs={{0,8},{4,12},{8,16},{12,20},{16,24},{20,28},{24,0},{28,4},{1,9},{5... | collective-permute-start | bytes 296 | tf_op jit(solution)/shard_map/ppermute | solution.py:290
  2.9 9.7 %collective-permute-start = (s32[24]{0:T(128)S(1)}, s32[24]{0:T(128)S(1)}, u32[]{:S(2)}, u32[]{:S(2)}) collective-permute-start(s32[24]{0:T(128)S(1)} %bitcast.31), channel_id=1, source_target_pairs={{0,4},{4,8},{8,12},{12,16},{16,20},{20,24},{24,28},{28,0},{1,5},{5... | collective-permute-start | bytes 296 | tf_op jit(solution)/shard_map/ppermute | solution.py:290
  4.3 8.3 %collective-permute-start.2 = (s32[24]{0:T(128)S(1)}, s32[24]{0:T(128)S(1)}, u32[]{:S(2)}, u32[]{:S(2)}) collective-permute-start(s32[24]{0:T(128)S(1)} %bitcast.32), channel_id=1, source_target_pairs={{0,28},{4,0},{8,4},{12,8},{16,12},{20,16},{24,20},{28,24},{1,29},{... | collective-permute-start | bytes 296 | tf_op jit(solution)/shard_map/ppermute | solution.py:290
  5.6 7.0 %collective-permute-start.3 = (s32[24]{0:T(128)S(1)}, s32[24]{0:T(128)S(1)}, u32[]{:S(2)}, u32[]{:S(2)}) collective-permute-start(s32[24]{0:T(128)S(1)} %bitcast.33), channel_id=1, source_target_pairs={{0,24},{4,28},{8,0},{12,4},{16,8},{20,12},{24,16},{28,20},{1,25},{... | collective-permute-start | bytes 296 | tf_op jit(solution)/shard_map/ppermute | solution.py:290
  118.1 4.1 %copy-start.2 = (f32[32,3072]{1,0:T(8,128)S(1)}, f32[32,3072]{1,0:T(8,128)}, u32[]{:S(2)}) copy-start(f32[32,3072]{1,0:T(8,128)} %get-tuple-element.9) | copy-start | bytes 1179652
  118.1 4.8 %copy-start.1 = (f32[32,3072]{1,0:T(8,128)S(1)}, f32[32,3072]{1,0:T(8,128)}, u32[]{:S(2)}) copy-start(f32[32,3072]{1,0:T(8,128)} %get-tuple-element.10) | copy-start | bytes 1179652

commit v2 on v1

--- a/solution.py
+++ b/solution.py
@@ -32,7 +32,7 @@
 def kernel(
     nw, nc, parts, total_rows,
     asked, near, search, values, rcols, rmine,
-    modes_out, resid_out, theta_out, grams_out,
+    modes_out, resid_out, theta_out, stiff_out, mass_out,
     stage, halo, others, st_hi, st_lo, image, part, got, gram, gram_got, gram_full, terms, terms_got,
     halo_send, halo_recv, all_send, all_recv, sum_send, sum_recv,
     red_send, red_recv, bc_send, bc_recv, th_send, th_recv,
@@ -44,7 +44,10 @@
     rows = blk * block
     span = rows // parts
     bspan = blk // parts
-    hspan = half // parts
+    extra = stage.shape[3] - width
+    per = width // extra
+    groups = half // (per + 1)
+    gspan = groups // parts
     chunk = gram_got.shape[2]
     owners = wide // chunk
     w = lax.axis_index("wire")
@@ -66,25 +69,45 @@
         pl.semaphore_signal(barrier, inc=1, device_id={"col": on_col(k)}, device_id_type=MESH)
 
     def fetch(t):
-        @pl.loop(t * hspan, (t + 1) * hspan)
-        def _(j):
+        @pl.loop(t * gspan, (t + 1) * gspan)
+        def _(g):
             for d in range(4):
-                stage[d, j] = search[asked[d, j]]
+                last = search[asked[d, g * (per + 1) + per]]
+                for m in range(per):
+                    stage[d, g * per + m] = jnp.concatenate(
+                        [search[asked[d, g * (per + 1) + m]], last[:, m * extra:(m + 1) * extra]], axis=1
+                    )
+
+    def fetched(d, g):
+        tiles = [halo[d, g * per + m] for m in range(per)]
+        return [tile[:, :width] for tile in tiles] + [
+            jnp.concatenate([tile[:, width:] for tile in tiles], axis=1)
+        ]
 
     def halo_copy(d, t):
-        js = pl.ds(t * hspan, hspan)
+        js = pl.ds(t * gspan * per, gspan * per)
         return remote(
             stage.at[d, js], halo.at[d, js], halo_send.at[d, t], halo_recv.at[d, t],
             {"wire": on_wire(-DISTANCES[d])},
         )
 
-    def all_copy(k):
-        return remote(search, others.at[c], all_send.at[k - 1], all_recv.at[k - 1], {"col": on_col(k)})
-
-    def all_arrival(k):
-        return remote(
-            search, others.at[on_col(-k)], all_send.at[k - 1], all_recv.at[k - 1], {"col": on_col(k)}
-        )
+    sibling = c + 1 - 2 * lax.rem(c, 2)
+
+    def all_copy(slot, way, t, device):
+        view = others.at[slot, :, pl.ds(t * span, span)]
+        return remote(view, view, all_send.at[way, t], all_recv.at[way, t], {"col": device})
+
+    def to_sibling(t):
+        return all_copy(c, 1, t, sibling)
+
+    def across(k, t):
+        return all_copy(c, k, t, on_col(k))
+
+    def forward(k, t):
+        return all_copy(on_col(-k), k + 1, t, sibling)
+
+    def arrival(slot, way, t):
+        return all_copy(slot, way, t, sibling)
 
     def sum_copy(k, t):
         ls = pl.ds(t * span, span)
@@ -120,39 +143,42 @@
         return remote(terms, terms_got.at[k], th_send.at[k], th_recv.at[k], {"wire": on_wire(k)})
 
     fetch(0)
-    others[c] = search[...]
     pl.semaphore_wait(barrier, nw + nc - 2)
     for t in range(parts):
         if t > 0:
             fetch(t)
         for d in (3, 1, 0, 2):
             halo_copy(d, t).start()
-    for k in range(1, nc):
-        all_copy(k).start()
-
-    def turn(q):
-        @pl.loop(0, parts)
-        def _(t):
-            at = others[q, pl.ds(t * bspan, bspan)].reshape(span, width).T
-            high, low = split(at)
-            ls = pl.ds(pl.multiple_of(t * span, 128), span)
-            rs = pl.ds(pl.multiple_of(q * width, 16), width)
-            st_hi[rs, ls] = high
-            st_lo[rs, ls] = low
-
-    turn(c)
-    for k in range(1, nc):
-        all_arrival(k).wait_recv()
-        turn(on_col(-k))
+        others[c, :, t * span:(t + 1) * span] = search[t * bspan:(t + 1) * bspan].reshape(span, width).T
+        for k in range(2, nc, 2):
+            across(k, t).start()
+        to_sibling(t).start()
+
+    for t in range(parts):
+        @pl.loop(t * bspan, (t + 1) * bspan)
+        def _(i):
+            mine = search[i]
+            picked = jnp.concatenate([mine, search[near[i]]], axis=0)
+            image[i] = 4.0 * mine + product(split(values[i][:, :2 * block]), split(picked))
+
+        for k in range(2, nc, 2):
+            arrival(on_col(-k), k, t).wait_recv()
+            forward(k, t).start()
 
     rc = split(rcols[...])
     gram[...] = jnp.zeros_like(gram)
 
-    @pl.loop(0, parts)
-    def _(t):
-        ls = pl.ds(pl.multiple_of(t * span, 128), span)
+    for t in range(parts):
+        ls = slice(t * span, (t + 1) * span)
+        arrival(sibling, 1, t).wait_recv()
+        for k in range(2, nc, 2):
+            arrival(lax.rem(sibling - k + nc, nc), k + 1, t).wait_recv()
+        for q in range(nc):
+            high, low = split(others[q, :, ls])
+            st_hi[q * width:(q + 1) * width, ls] = high
+            st_lo[q * width:(q + 1) * width, ls] = low
         here = (st_hi[:, ls], st_lo[:, ls])
-        own = split(search[pl.ds(t * bspan, bspan)].reshape(span, width))
+        own = split(search[t * bspan:(t + 1) * bspan].reshape(span, width))
         gram[1] += product(here, own)
         modes_out[:, ls] = product(rc, here)
 
@@ -163,14 +189,14 @@
         for d in range(4):
             halo_copy(d, t).wait_recv()
 
-        @pl.loop(t * hspan, (t + 1) * hspan)
-        def _(j):
+        @pl.loop(t * gspan, (t + 1) * gspan)
+        def _(g):
             for odd in range(2):
-                i = 2 * j + odd
-                picked = jnp.concatenate(
-                    [search[i], search[near[i]], halo[2 * odd, j], halo[2 * odd + 1, j]], axis=0
-                )
-                image[i] = 4.0 * search[i] + product(split(values[i]), split(picked))
+                pieces = zip(fetched(2 * odd, g), fetched(2 * odd + 1, g))
+                for m, pair in enumerate(pieces):
+                    i = 2 * (g * (per + 1) + m) + odd
+                    picked = jnp.concatenate(pair, axis=0)
+                    image[i] += product(split(values[i][:, 2 * block:]), split(picked))
 
         img = split(image[t * bspan:(t + 1) * bspan].reshape(span, width))
         turned = product(rm, img, NT)
@@ -258,14 +284,18 @@
                 red_copy(0, k).wait_send()
                 red_copy(1, k).wait_send()
 
-    grams_out[...] = gram_full[...]
+    stiff_out[...] = gram_full[0]
+    mass_out[...] = gram_full[1]
     for t in range(parts):
         for d in range(4):
             halo_copy(d, t).wait_send()
         for k in range(1, nc):
             sum_copy(k, t).wait_send()
-    for k in range(1, nc):
-        all_copy(k).wait_send()
+    for t in range(parts):
+        to_sibling(t).wait_send()
+        for k in range(2, nc, 2):
+            across(k, t).wait_send()
+            forward(k, t).wait_send()
 
 
 def shards(search, block_values, block_cols, ritz):
@@ -278,7 +308,11 @@
     nw, nc = lax.axis_size("wire"), lax.axis_size("col")
     mc = modes // nc
     c = lax.axis_index("col")
-    parts = next(n for n in (3, 2, 1) if half % n == 0 and (rows // n) % 128 == 0)
+    extra = -width % 128
+    per = width // extra
+    assert width % extra == 0 and half % (per + 1) == 0 and nc % 2 == 0
+    groups = half // (per + 1)
+    parts = next(n for n in (3, 2, 1) if groups % n == 0 and (rows // n) % 128 == 0)
     chunk = max(8, -(-wide // nw) // 8 * 8)
     assert wide % chunk == 0 and wide // chunk <= nw
     owners = wide // chunk
@@ -295,20 +329,21 @@
     vmem = pl.BlockSpec(memory_space=pltpu.VMEM)
     smem = pl.BlockSpec(memory_space=pltpu.SMEM)
     dma = pltpu.SemaphoreType.DMA
-    modes_t, resid_t, theta, grams = pl.pallas_call(
+    modes_t, resid_t, theta, stiff, mass = pl.pallas_call(
         functools.partial(kernel, nw, nc, parts, float(rows * nw)),
         out_shape=(
             jax.ShapeDtypeStruct((mc, rows), f32),
             jax.ShapeDtypeStruct((mc, rows), f32),
             jax.ShapeDtypeStruct((mc, 128), f32),
-            jax.ShapeDtypeStruct((2, wide, width), f32),
+            jax.ShapeDtypeStruct((wide, width), f32),
+            jax.ShapeDtypeStruct((wide, width), f32),
         ),
         in_specs=[smem, smem, vmem, vmem, vmem, vmem],
-        out_specs=(vmem,) * 4,
+        out_specs=(vmem,) * 5,
         scratch_shapes=[
-            pltpu.VMEM((4, half, block, width), f32),
-            pltpu.VMEM((4, half, block, width), f32),
-            pltpu.VMEM((nc, blk, block, width), f32),
+            pltpu.VMEM((4, groups * per, block, width + extra), f32),
+            pltpu.VMEM((4, groups * per, block, width + extra), f32),
+            pltpu.VMEM((nc, width, rows), f32),
             pltpu.VMEM((wide, rows), jnp.bfloat16),
             pltpu.VMEM((wide, rows), jnp.bfloat16),
             pltpu.VMEM((blk, block, width), f32),
@@ -320,7 +355,7 @@
             pltpu.VMEM((mc, 128), f32),
             pltpu.VMEM((nw, mc, 128), f32),
             dma((4, parts)), dma((4, parts)),
-            dma((nc - 1,)), dma((nc - 1,)),
+            dma((nc, parts)), dma((nc, parts)),
             dma((nc - 1, parts)), dma((nc - 1, parts)),
             dma((2, nw)), dma((2, nw)),
             dma((nw,)), dma((nw,)),
@@ -332,7 +367,7 @@
         name="step",
     )(asked, local[:, 1], search.reshape(blk, block, width),
       block_values.reshape(blk, block, slots * block), rcols, rmine)
-    return modes_t.T, resid_t.T, theta[:, 0], grams[0], grams[1]
+    return modes_t.T, resid_t.T, theta[:, 0], stiff, mass
 
 
 def solution(mesh):

time: 124 us -> 90.3 us (0.73)
  Pallas kernels: 105 us -> 68.9 us
  local copies, waits for them, and re-layouts: 11 us -> 12.8 us
    pallas_call x1, Pallas kernels: 105 us -> 68.9 us  [shards(): pl.pallas_call(functools.partial(kernel, nw, nc, parts, float(rows * nw))...]
    unnamed x13 -> x11, local copies, waits for them, and re-layouts: 7.44 us -> 10.3 us
  transfers between devices with their start and end apart: 4 -> 4, of which waited for: 0 -> 0; matrix products, arithmetic and copies ran while one was open for 4% -> 6% of each run, Pallas kernels for 0% -> 0%
where the time goes in v2:
time: 90.3 us; the launch traced here: 89.6 us
  Pallas kernels  68.9 us (76%)
  local copies, waits for them, and re-layouts  12.8 us (14%)
  starting transfers between devices  5.83 us (6%)
  other arithmetic  1.32 us (1%)
    pallas_call x1, Pallas kernels, shards(): pl.pallas_call(functools.partial(kernel, nw, nc, parts, float(rows * nw))...  68.9 us
    unnamed x11, local copies, waits for them, and re-layouts  10.3 us
    ppermute x4, starting transfers between devices, shards(): lax.ppermute(wanted, 'wire', [(i, (i + distance) % nw) for i in range(nw)])  5.83 us
  transfers between devices with their start and end apart: 4, of which 0 were waited for; matrix products, arithmetic and copies ran while one was open for 6% of the time, Pallas kernels for 0%

profile of v2, /device:TPU:9, one launch (start us, length us, event | category | flops | bytes accessed | tf_op | source)
XLA Modules:
  0.0 89.6 jit_solution(14121721392868838378)
XLA Ops:
  0.6 0.0 copy-start
  0.6 0.7 add_select_fusion
  1.4 0.1 slice.19
  1.5 1.3 %collective-permute-start.1 = (s32[24]{0:T(128)S(1)}, s32[24]{0:T(128)S(1)}, u32[]{:S(2)}, u32[]{:S(2)}) collective-permute-start(s32[24]{0:T(128)S(1)} %bitcast.26), channel_id=1, source_target_pairs={{0,8},{4,12},{8,16},{12,20},{16,24},{20,28},{24,0},{28,4},{1,9},{5... | collective-permute-start | bytes 296 | tf_op jit(solution)/shard_map/ppermute | solution.py:324
  2.8 0.1 slice.18
  2.9 1.3 %collective-permute-start = (s32[24]{0:T(128)S(1)}, s32[24]{0:T(128)S(1)}, u32[]{:S(2)}, u32[]{:S(2)}) collective-permute-start(s32[24]{0:T(128)S(1)} %bitcast.27), channel_id=1, source_target_pairs={{0,4},{4,8},{8,12},{12,16},{16,20},{20,24},{24,28},{28,0},{1,5},{5... | collective-permute-start | bytes 296 | tf_op jit(solution)/shard_map/ppermute | solution.py:324
  4.2 0.1 slice.20
  4.3 1.2 %collective-permute-start.2 = (s32[24]{0:T(128)S(1)}, s32[24]{0:T(128)S(1)}, u32[]{:S(2)}, u32[]{:S(2)}) collective-permute-start(s32[24]{0:T(128)S(1)} %bitcast.28), channel_id=1, source_target_pairs={{0,28},{4,0},{8,4},{12,8},{16,12},{20,16},{24,20},{28,24},{1,29},{... | collective-permute-start | bytes 296 | tf_op jit(solution)/shard_map/ppermute | solution.py:324
  5.5 0.1 slice.21
  5.6 2.0 %collective-permute-start.3 = (s32[24]{0:T(128)S(1)}, s32[24]{0:T(128)S(1)}, u32[]{:S(2)}, u32[]{:S(2)}) collective-permute-start(s32[24]{0:T(128)S(1)} %bitcast.29), channel_id=1, source_target_pairs={{0,24},{4,28},{8,0},{12,4},{16,8},{20,12},{24,16},{28,20},{1,25},{... | collective-permute-start | bytes 296 | tf_op jit(solution)/shard_map/ppermute | solution.py:324
  7.7 0.5 slice_bitcast_fusion.near
  8.2 0.0 copy-done
  8.2 0.7 copy.20
  8.9 0.1 constant_dynamic-slice_fusion.1
  9.0 0.7 copy.19
  9.8 2.9 %copy.14 = f32[3072,96]{1,0:T(8,128)} copy(f32[3072,96]{0,1:T(8,128)} %param.4) | data formatting | bytes 2359296 | tf_op args[0]
  12.7 0.0 collective-permute-done.1
  12.7 0.0 collective-permute-done
  12.7 0.0 collective-permute-done.2
  12.7 0.0 collective-permute-done.3
  12.7 0.6 pad_add_fusion.asked
  13.3 68.9 %step.1 = (f32[32,3072]{1,0:T(8,128)}, f32[32,3072]{1,0:T(8,128)}, f32[32,128]{1,0:T(8,128)}, f32[384,96]{1,0:T(8,128)}, f32[384,96]{1,0:T(8,128)}) custom-call(s32[4,24]{1,0:T(4,128)} %pad_add_fusion.asked, s32[48]{0:T(128)} %slice_bitcast_fusion.near, f32[48,64,96]{2,1,0:T(8,128)} %bitcast.16, f32[48,64,256]{2,1,0:T(8,128)} %bitcast.17, ...), custom_call_target="tpu_custom_call" | custom-call | tf_op jit(solution)/shard_map/step/pallas_call | solution.py:332
  82.2 0.0 copy-start.1
  82.2 1.4 %slice_reduce_fusion = f32[32]{0:T(128)} fusion(f32[32,128]{1,0:T(8,128)} %get-tuple-element.12), kind=kLoop, calls=%fused_computation | loop fusion | bytes 256 | tf_op jit(solution)/shard_map/slice | solution.py:370
  83.6 1.7 %copy.17 = f32[384,96]{0,1:T(8,128)} copy(f32[384,96]{1,0:T(8,128)} %get-tuple-element.23) | data formatting | bytes 294912
  85.3 1.7 %copy.18 = f32[384,96]{0,1:T(8,128)} copy(f32[384,96]{1,0:T(8,128)} %get-tuple-element.24) | data formatting | bytes 294912
  87.0 1.8 %copy.23 = f32[3072,32]{0,1:T(8,128)} copy(f32[3072,32]{0,1:T(8,128)} %bitcast.19) | data formatting | bytes 786432
  88.8 0.0 copy-done.1
  88.8 0.7 copy.24
  (1 shorter events, 0.0 us)
Async XLA Ops:
  0.6 7.5 %copy-start = (f32[384,128]{1,0:T(8,128)S(1)}, f32[384,128]{1,0:T(8,128)}, u32[]{:S(2)}) copy-start(f32[384,128]{1,0:T(8,128)} %param.7) | copy-start | bytes 589828
  1.5 11.2 %collective-permute-start.1 = (s32[24]{0:T(128)S(1)}, s32[24]{0:T(128)S(1)}, u32[]{:S(2)}, u32[]{:S(2)}) collective-permute-start(s32[24]{0:T(128)S(1)} %bitcast.26), channel_id=1, source_target_pairs={{0,8},{4,12},{8,16},{12,20},{16,24},{20,28},{24,0},{28,4},{1,9},{5... | collective-permute-start | bytes 296 | tf_op jit(solution)/shard_map/ppermute | solution.py:324
  2.9 9.7 %collective-permute-start = (s32[24]{0:T(128)S(1)}, s32[24]{0:T(128)S(1)}, u32[]{:S(2)}, u32[]{:S(2)}) collective-permute-start(s32[24]{0:T(128)S(1)} %bitcast.27), channel_id=1, source_target_pairs={{0,4},{4,8},{8,12},{12,16},{16,20},{20,24},{24,28},{28,0},{1,5},{5... | collective-permute-start | bytes 296 | tf_op jit(solution)/shard_map/ppermute | solution.py:324
  4.3 8.3 %collective-permute-start.2 = (s32[24]{0:T(128)S(1)}, s32[24]{0:T(128)S(1)}, u32[]{:S(2)}, u32[]{:S(2)}) collective-permute-start(s32[24]{0:T(128)S(1)} %bitcast.28), channel_id=1, source_target_pairs={{0,28},{4,0},{8,4},{12,8},{16,12},{20,16},{24,20},{28,24},{1,29},{... | collective-permute-start | bytes 296 | tf_op jit(solution)/shard_map/ppermute | solution.py:324
  5.6 7.0 %collective-permute-start.3 = (s32[24]{0:T(128)S(1)}, s32[24]{0:T(128)S(1)}, u32[]{:S(2)}, u32[]{:S(2)}) collective-permute-start(s32[24]{0:T(128)S(1)} %bitcast.29), channel_id=1, source_target_pairs={{0,24},{4,28},{8,0},{12,4},{16,8},{20,12},{24,16},{28,20},{1,25},{... | collective-permute-start | bytes 296 | tf_op jit(solution)/shard_map/ppermute | solution.py:324
  82.2 6.6 %copy-start.1 = (f32[32,3072]{1,0:T(8,128)S(1)}, f32[32,3072]{1,0:T(8,128)}, u32[]{:S(2)}) copy-start(f32[32,3072]{1,0:T(8,128)} %get-tuple-element.11) | copy-start | bytes 1179652

commit v3 on v2

--- a/solution.py
+++ b/solution.py
@@ -31,16 +31,16 @@
 
 def kernel(
     nw, nc, parts, total_rows,
-    asked, near, search, values, rcols, rmine,
+    named, wanted, search_t, values, ritz,
     modes_out, resid_out, theta_out, stiff_out, mass_out,
-    stage, halo, others, st_hi, st_lo, image, part, got, gram, gram_got, gram_full, terms, terms_got,
-    halo_send, halo_recv, all_send, all_recv, sum_send, sum_recv,
+    search, ritz_t, requests, asked, stage, halo, others, st_hi, st_lo, image, part, got, gram, gram_got, gram_full, terms, terms_got,
+    ask_send, ask_recv, ask_local, halo_send, halo_recv, all_send, all_recv, sum_send, sum_recv,
     red_send, red_recv, bc_send, bc_recv, th_send, th_recv,
 ):
     blk, block, width = search.shape
     half = blk // 2
     wide = gram.shape[1]
-    mc = rcols.shape[0]
+    mc = modes_out.shape[0]
     rows = blk * block
     span = rows // parts
     bspan = blk // parts
@@ -68,14 +68,17 @@
     for k in range(1, nc):
         pl.semaphore_signal(barrier, inc=1, device_id={"col": on_col(k)}, device_id_type=MESH)
 
+    def requested(d, j):
+        return search[lax.rem(asked[d, 2 + d % 2, 2 * j + d // 2], blk)]
+
     def fetch(t):
         @pl.loop(t * gspan, (t + 1) * gspan)
         def _(g):
             for d in range(4):
-                last = search[asked[d, g * (per + 1) + per]]
+                last = requested(d, g * (per + 1) + per)
                 for m in range(per):
                     stage[d, g * per + m] = jnp.concatenate(
-                        [search[asked[d, g * (per + 1) + m]], last[:, m * extra:(m + 1) * extra]], axis=1
+                        [requested(d, g * (per + 1) + m), last[:, m * extra:(m + 1) * extra]], axis=1
                     )
 
     def fetched(d, g):
@@ -83,6 +86,11 @@
         return [tile[:, :width] for tile in tiles] + [
             jnp.concatenate([tile[:, width:] for tile in tiles], axis=1)
         ]
+
+    def ask_copy(d):
+        return remote(
+            wanted, requests.at[d], ask_send.at[d], ask_recv.at[d], {"wire": on_wire(DISTANCES[d])}
+        )
 
     def halo_copy(d, t):
         js = pl.ds(t * gspan * per, gspan * per)
@@ -93,15 +101,16 @@
 
     sibling = c + 1 - 2 * lax.rem(c, 2)
 
-    def all_copy(slot, way, t, device):
+    def all_copy(slot, way, t, device, own=False):
         view = others.at[slot, :, pl.ds(t * span, span)]
-        return remote(view, view, all_send.at[way, t], all_recv.at[way, t], {"col": device})
+        src = search_t.at[:, pl.ds(t * span, span)] if own else view
+        return remote(src, view, all_send.at[way, t], all_recv.at[way, t], {"col": device})
 
     def to_sibling(t):
-        return all_copy(c, 1, t, sibling)
+        return all_copy(c, 1, t, sibling, True)
 
     def across(k, t):
-        return all_copy(c, k, t, on_col(k))
+        return all_copy(c, k, t, on_col(k), True)
 
     def forward(k, t):
         return all_copy(on_col(-k), k + 1, t, sibling)
@@ -142,30 +151,40 @@
     def th_copy(k):
         return remote(terms, terms_got.at[k], th_send.at[k], th_recv.at[k], {"wire": on_wire(k)})
 
-    fetch(0)
     pl.semaphore_wait(barrier, nw + nc - 2)
-    for t in range(parts):
-        if t > 0:
-            fetch(t)
-        for d in (3, 1, 0, 2):
-            halo_copy(d, t).start()
-        others[c, :, t * span:(t + 1) * span] = search[t * bspan:(t + 1) * bspan].reshape(span, width).T
+    for d in range(4):
+        ask_copy(d).start()
+    for t in range(parts):
         for k in range(2, nc, 2):
             across(k, t).start()
         to_sibling(t).start()
+    for t in range(parts):
+        turned = search_t[:, t * span:(t + 1) * span].T
+        search[t * bspan:(t + 1) * bspan] = turned.reshape(bspan, block, width)
+    for d in range(4):
+        ask_copy(d).wait_recv()
+    down = pltpu.make_async_copy(requests, asked, ask_local)
+    down.start()
+    down.wait()
+    for t in range(parts):
+        fetch(t)
+        for d in (3, 1, 0, 2):
+            halo_copy(d, t).start()
+    others[c] = search_t[...]
+    ritz_t[...] = ritz[...].T
 
     for t in range(parts):
         @pl.loop(t * bspan, (t + 1) * bspan)
         def _(i):
             mine = search[i]
-            picked = jnp.concatenate([mine, search[near[i]]], axis=0)
+            picked = jnp.concatenate([mine, search[lax.rem(named[1, i], blk)]], axis=0)
             image[i] = 4.0 * mine + product(split(values[i][:, :2 * block]), split(picked))
 
         for k in range(2, nc, 2):
             arrival(on_col(-k), k, t).wait_recv()
             forward(k, t).start()
 
-    rc = split(rcols[...])
+    rc = split(ritz_t[pl.ds(pl.multiple_of(c * mc, 8), mc)])
     gram[...] = jnp.zeros_like(gram)
 
     for t in range(parts):
@@ -184,7 +203,7 @@
 
     start_red(1)
 
-    rm = split(rmine[...])
+    rm = split(ritz[pl.ds(pl.multiple_of(c * width, 8), width)].T)
     for t in range(parts):
         for d in range(4):
             halo_copy(d, t).wait_recv()
@@ -259,7 +278,7 @@
 
     sums = terms_got[0]
     theta = sums[:, 0:1] / sums[:, 64:65]
-    theta_out[...] = jnp.broadcast_to(theta, theta_out.shape)
+    theta_out[...] = jnp.broadcast_to(theta, terms.shape).T[:theta_out.shape[0]]
     resid_out[...] = resid_out[...] - modes_out[...] * theta
 
     @pl.loop(1, nw)
@@ -284,8 +303,10 @@
                 red_copy(0, k).wait_send()
                 red_copy(1, k).wait_send()
 
-    stiff_out[...] = gram_full[0]
-    mass_out[...] = gram_full[1]
+    stiff_out[...] = gram_full[0].T
+    mass_out[...] = gram_full[1].T
+    for d in range(4):
+        ask_copy(d).wait_send()
     for t in range(parts):
         for d in range(4):
             halo_copy(d, t).wait_send()
@@ -307,7 +328,6 @@
     wide, modes = ritz.shape
     nw, nc = lax.axis_size("wire"), lax.axis_size("col")
     mc = modes // nc
-    c = lax.axis_index("col")
     extra = -width % 128
     per = width // extra
     assert width % extra == 0 and half % (per + 1) == 0 and nc % 2 == 0
@@ -316,15 +336,7 @@
     chunk = max(8, -(-wide // nw) // 8 * 8)
     assert wide % chunk == 0 and wide // chunk <= nw
     owners = wide // chunk
-    local = block_cols % blk
-    asked = []
-    for distance, wanted in zip(
-        DISTANCES, (local[0::2, 2], local[0::2, 3], local[1::2, 2], local[1::2, 3])
-    ):
-        asked.append(lax.ppermute(wanted, "wire", [(i, (i + distance) % nw) for i in range(nw)]))
-    asked = jnp.stack(asked)
-    rcols = lax.dynamic_slice_in_dim(ritz, c * mc, mc, 1).T
-    rmine = lax.dynamic_slice_in_dim(ritz, c * width, width, 0).T
+    wanted = jnp.pad(block_cols.T, ((0, -slots % 8), (0, -blk % 128)))
     f32 = jnp.float32
     vmem = pl.BlockSpec(memory_space=pltpu.VMEM)
     smem = pl.BlockSpec(memory_space=pltpu.SMEM)
@@ -334,13 +346,17 @@
         out_shape=(
             jax.ShapeDtypeStruct((mc, rows), f32),
             jax.ShapeDtypeStruct((mc, rows), f32),
-            jax.ShapeDtypeStruct((mc, 128), f32),
-            jax.ShapeDtypeStruct((wide, width), f32),
-            jax.ShapeDtypeStruct((wide, width), f32),
+            jax.ShapeDtypeStruct((8, mc), f32),
+            jax.ShapeDtypeStruct((width, wide), f32),
+            jax.ShapeDtypeStruct((width, wide), f32),
         ),
-        in_specs=[smem, smem, vmem, vmem, vmem, vmem],
+        in_specs=[smem, vmem, vmem, vmem, vmem],
         out_specs=(vmem,) * 5,
         scratch_shapes=[
+            pltpu.VMEM((blk, block, width), f32),
+            pltpu.VMEM((modes, wide), f32),
+            pltpu.VMEM((4, *wanted.shape), jnp.int32),
+            pltpu.SMEM((4, *wanted.shape), jnp.int32),
             pltpu.VMEM((4, groups * per, block, width + extra), f32),
             pltpu.VMEM((4, groups * per, block, width + extra), f32),
             pltpu.VMEM((nc, width, rows), f32),
@@ -354,6 +370,7 @@
             pltpu.VMEM((2, wide, width), f32),
             pltpu.VMEM((mc, 128), f32),
             pltpu.VMEM((nw, mc, 128), f32),
+            dma((4,)), dma((4,)), dma,
             dma((4, parts)), dma((4, parts)),
             dma((nc, parts)), dma((nc, parts)),
             dma((nc - 1, parts)), dma((nc - 1, parts)),
@@ -365,9 +382,8 @@
             collective_id=0, has_side_effects=True, vmem_limit_bytes=56 * 1024 * 1024
         ),
         name="step",
-    )(asked, local[:, 1], search.reshape(blk, block, width),
-      block_values.reshape(blk, block, slots * block), rcols, rmine)
-    return modes_t.T, resid_t.T, theta[:, 0], stiff, mass
+    )(wanted, wanted, search.T, block_values.reshape(blk, block, slots * block), ritz)
+    return modes_t.T, resid_t.T, theta[0], stiff.T, mass.T
 
 
 def solution(mesh):

time: 90.3 us -> 83.8 us (0.928)
  starting transfers between devices: 5.83 us -> 0 us
  Pallas kernels: 68.9 us -> 73.7 us
  local copies, waits for them, and re-layouts: 12.8 us -> 9.16 us
  other arithmetic: 1.32 us -> 0 us
    ppermute x4 -> x0, starting transfers between devices: 5.83 us -> none  [shards(): lax.ppermute(wanted, 'wire', [(i, (i + distance) % nw) for i in range(nw)])]
    pallas_call x1, Pallas kernels: 68.9 us -> 73.7 us  [shards(): pl.pallas_call(functools.partial(kernel, nw, nc, parts, float(rows * nw))...]
    unnamed x11 -> x4, local copies, waits for them, and re-layouts: 10.3 us -> 6.69 us
    slice x5 -> x0, local copies, waits for them, and re-layouts: 1.83 us -> none  [the longest x1 1.39 us: shards(): return (modes_t.T, resid_t.T, theta[:, 0], stiff, mass)]
    pad x0 -> x1, local copies, waits for them, and re-layouts: none -> 1.28 us  [shards(): wanted = jnp.pad(block_cols.T, ((0, -slots % 8), (0, -blk % 128)))]
  transfers between devices with their start and end apart: 4 -> 0, of which waited for: 0 -> 0; matrix products, arithmetic and copies ran while one was open for 6% -> 0% of each run, Pallas kernels for 0% -> 0%
where the time goes in v3:
time: 83.8 us; the launch traced here: 83.5 us
  Pallas kernels  73.7 us (88%)
  local copies, waits for them, and re-layouts  9.16 us (11%)
    pallas_call x1, Pallas kernels, shards(): pl.pallas_call(functools.partial(kernel, nw, nc, parts, float(rows * nw))...  73.7 us
    unnamed x4, local copies, waits for them, and re-layouts  6.69 us

profile of v3, /device:TPU:9, one launch (start us, length us, event | category | flops | bytes accessed | tf_op | source)
XLA Modules:
  0.0 83.5 jit_solution(12015362248283733999)
XLA Ops:
  0.6 1.3 %pad.4.named.wanted = s32[8,128]{1,0:T(8,128)} pad(s32[4,48]{1,0:T(4,128)} %bitcast.15, s32[]{:T(128)} %constant.0.clone.1), padding=0_4x0_80 | pad | bytes 4868 | tf_op jit(solution)/shard_map/jit(_pad)/pad | solution.py:339
  1.9 73.7 %step.1 = (f32[32,3072]{1,0:T(8,128)}, f32[32,3072]{1,0:T(8,128)}, f32[8,32]{1,0:T(8,128)}, f32[96,384]{1,0:T(8,128)}, f32[96,384]{1,0:T(8,128)}) custom-call(s32[8,128]{1,0:T(8,128)} %pad.4.named.wanted, s32[8,128]{1,0:T(8,128)} %pad.4.named.wanted, f32[96,3072]{1,0:T(8,128)} %bitcast.10, f32[48,64,256]{2,1,0:T(8,128)} %bitcast.9, f32[384,128]{1,0:T(8,128)} %ritz.1), custom_call_target="tpu_custom_call" | custom-call | tf_op jit(solution)/shard_map/step/pallas_call | solution.py:344
  75.6 1.2 %slice_bitcast_fusion = f32[32]{0:T(128)} fusion(f32[8,32]{1,0:T(8,128)} %get-tuple-element.12), kind=kLoop, calls=%fused_computation | loop fusion | bytes 256 | tf_op jit(solution)/shard_map/squeeze | solution.py:386
  76.8 1.8 %copy.13 = f32[3072,32]{0,1:T(8,128)} copy(f32[3072,32]{0,1:T(8,128)} %bitcast.12) | data formatting | bytes 786432
  78.5 1.8 %copy.14 = f32[3072,32]{0,1:T(8,128)} copy(f32[3072,32]{0,1:T(8,128)} %bitcast.11) | data formatting | bytes 786432
  80.3 1.6 %copy.15 = f32[384,96]{0,1:T(8,128)} copy(f32[384,96]{0,1:T(8,128)} %bitcast.14) | data formatting | bytes 294912
  81.9 1.6 %copy.16 = f32[384,96]{0,1:T(8,128)} copy(f32[384,96]{0,1:T(8,128)} %bitcast.13) | data formatting | bytes 294912

commit v4 on v3

--- a/solution.py
+++ b/solution.py
@@ -32,7 +32,7 @@
 def kernel(
     nw, nc, parts, total_rows,
     named, wanted, search_t, values, ritz,
-    modes_out, resid_out, theta_out, stiff_out, mass_out,
+    modes_out, image_out, theta_out, stiff_out, mass_out,
     search, ritz_t, requests, asked, stage, halo, others, st_hi, st_lo, image, part, got, gram, gram_got, gram_full, terms, terms_got,
     ask_send, ask_recv, ask_local, halo_send, halo_recv, all_send, all_recv, sum_send, sum_recv,
     red_send, red_recv, bc_send, bc_recv, th_send, th_recv,
@@ -237,7 +237,7 @@
         mine = part[c, :, ls]
         for k in range(1, nc):
             mine = mine + got[k - 1, :, ls]
-        resid_out[:, ls] = mine
+        image_out[:, ls] = mine
         modes = modes_out[:, ls]
         numer = numer + jnp.sum(modes * mine, axis=1, keepdims=True)
         denom = denom + jnp.sum(modes * modes, axis=1, keepdims=True)
@@ -278,8 +278,7 @@
 
     sums = terms_got[0]
     theta = sums[:, 0:1] / sums[:, 64:65]
-    theta_out[...] = jnp.broadcast_to(theta, terms.shape).T[:theta_out.shape[0]]
-    resid_out[...] = resid_out[...] - modes_out[...] * theta
+    theta_out[...] = jnp.broadcast_to(theta, terms.shape)
 
     @pl.loop(1, nw)
     def _(k):
@@ -317,6 +316,14 @@
         for k in range(2, nc, 2):
             across(k, t).wait_send()
             forward(k, t).wait_send()
+
+
+def finish(modes, image, theta, stiff, mass, modes_out, resid_out, theta_out, stiff_out, mass_out):
+    modes_out[...] = modes[...]
+    resid_out[...] = image[...] - modes[...] * theta[:, 0:1]
+    theta_out[...] = theta[...].T[0]
+    stiff_out[...] = stiff[...]
+    mass_out[...] = mass[...]
 
 
 def shards(search, block_values, block_cols, ritz):
@@ -332,7 +339,7 @@
     per = width // extra
     assert width % extra == 0 and half % (per + 1) == 0 and nc % 2 == 0
     groups = half // (per + 1)
-    parts = next(n for n in (3, 2, 1) if groups % n == 0 and (rows // n) % 128 == 0)
+    parts = next(n for n in (6, 3, 2, 1) if groups % n == 0 and (rows // n) % 128 == 0)
     chunk = max(8, -(-wide // nw) // 8 * 8)
     assert wide % chunk == 0 and wide // chunk <= nw
     owners = wide // chunk
@@ -341,12 +348,12 @@
     vmem = pl.BlockSpec(memory_space=pltpu.VMEM)
     smem = pl.BlockSpec(memory_space=pltpu.SMEM)
     dma = pltpu.SemaphoreType.DMA
-    modes_t, resid_t, theta, stiff, mass = pl.pallas_call(
+    results = pl.pallas_call(
         functools.partial(kernel, nw, nc, parts, float(rows * nw)),
         out_shape=(
             jax.ShapeDtypeStruct((mc, rows), f32),
             jax.ShapeDtypeStruct((mc, rows), f32),
-            jax.ShapeDtypeStruct((8, mc), f32),
+            jax.ShapeDtypeStruct((mc, 128), f32),
             jax.ShapeDtypeStruct((width, wide), f32),
             jax.ShapeDtypeStruct((width, wide), f32),
         ),
@@ -383,7 +390,18 @@
         ),
         name="step",
     )(wanted, wanted, search.T, block_values.reshape(blk, block, slots * block), ritz)
-    return modes_t.T, resid_t.T, theta[0], stiff.T, mass.T
+    modes_t, resid_t, theta, stiff, mass = pl.pallas_call(
+        finish,
+        out_shape=tuple(
+            jax.ShapeDtypeStruct(shape, f32)
+            for shape in ((mc, rows), (mc, rows), (mc,), (width, wide), (width, wide))
+        ),
+        in_specs=[vmem] * 5,
+        out_specs=(vmem,) * 5,
+        compiler_params=pltpu.CompilerParams(vmem_limit_bytes=16 * 1024 * 1024),
+        name="finish",
+    )(*results)
+    return modes_t.T, resid_t.T, theta, stiff.T, mass.T
 
 
 def solution(mesh):

time: 83.8 us -> 80.7 us (0.963)
  local copies, waits for them, and re-layouts: 9.16 us -> 5.8 us
    unnamed x4 -> x10, local copies, waits for them, and re-layouts: 6.69 us -> 4.52 us
    squeeze x1 -> x0, local copies, waits for them, and re-layouts: 1.19 us -> none  [shards(): return (modes_t.T, resid_t.T, theta[0], stiff.T, mass.T)]
    pallas_call x0 -> x1, Pallas kernels: none -> 1.02 us  [shards(): pl.pallas_call(finish, out_shape=tuple((jax.ShapeDtypeStruct(shape, f32)...]
where the time goes in v4:
time: 80.7 us; the launch traced here: 80.3 us
  Pallas kernels  73.9 us (92%)
  local copies, waits for them, and re-layouts  5.8 us (7%)
    pallas_call x1, Pallas kernels, shards(): pl.pallas_call(functools.partial(kernel, nw, nc, parts, float(rows * nw))...  72.8 us
    unnamed x10, local copies, waits for them, and re-layouts  4.52 us

profile of v4, /device:TPU:9, one launch (start us, length us, event | category | flops | bytes accessed | tf_op | source)
XLA Modules:
  0.0 80.3 jit_solution(15398519719674547550)
XLA Ops:
  0.6 1.3 %pad.4.named.wanted = s32[8,128]{1,0:T(8,128)} pad(s32[4,48]{1,0:T(4,128)} %bitcast.9, s32[]{:T(128)} %constant.0.clone.1), padding=0_4x0_80 | pad | bytes 4868 | tf_op jit(solution)/shard_map/jit(_pad)/pad | solution.py:346
  1.9 72.8 %step.1 = (f32[32,3072]{1,0:T(8,128)}, f32[32,3072]{1,0:T(8,128)}, f32[32,128]{1,0:T(8,128)}, f32[96,384]{1,0:T(8,128)}, f32[96,384]{1,0:T(8,128)}) custom-call(s32[8,128]{1,0:T(8,128)} %pad.4.named.wanted, s32[8,128]{1,0:T(8,128)} %pad.4.named.wanted, f32[96,3072]{1,0:T(8,128)} %bitcast.8, f32[48,64,256]{2,1,0:T(8,128)} %bitcast.7, f32[384,128]{1,0:T(8,128)} %ritz.1), custom_call_target="tpu_custom_call" | custom-call | tf_op jit(solution)/shard_map/step/pallas_call | solution.py:351
  74.8 0.0 copy-start
  74.8 1.0 %copy-done = f32[32,3072]{1,0:T(8,128)S(1)} copy-done((f32[32,3072]{1,0:T(8,128)S(1)}, f32[32,3072]{1,0:T(8,128)}, u32[]{:S(2)}) %copy-start) | copy-done | bytes 393240
  75.8 0.0 copy-start.1
  75.8 1.0 %copy-done.1 = f32[32,3072]{1,0:T(8,128)S(1)} copy-done((f32[32,3072]{1,0:T(8,128)S(1)}, f32[32,3072]{1,0:T(8,128)}, u32[]{:S(2)}) %copy-start.1) | copy-done | bytes 393240
  76.7 0.0 copy-start.2
  76.8 0.9 %copy-done.2 = f32[96,384]{1,0:T(8,128)S(1)} copy-done((f32[96,384]{1,0:T(8,128)S(1)}, f32[96,384]{1,0:T(8,128)}, u32[]{:S(2)}) %copy-start.2) | copy-done | bytes 147480
  77.7 0.0 copy-start.3
  77.7 0.9 %copy-done.3 = f32[96,384]{1,0:T(8,128)S(1)} copy-done((f32[96,384]{1,0:T(8,128)S(1)}, f32[96,384]{1,0:T(8,128)}, u32[]{:S(2)}) %copy-start.3) | copy-done | bytes 147480
  78.6 0.0 copy-start.4
  78.6 0.7 copy-done.4
  79.3 1.0 %finish.1 = (f32[32,3072]{1,0:T(8,128)}, f32[32,3072]{1,0:T(8,128)}, f32[32]{0:T(128)}, f32[96,384]{1,0:T(8,128)}, f32[96,384]{1,0:T(8,128)}) custom-call(f32[32,3072]{1,0:T(8,128)S(1)} %copy-done, f32[32,3072]{1,0:T(8,128)S(1)} %copy-done.1, f32[32,128]{1,0:T(8,128)S(1)} %copy-done.4, f32[96,384]{1,0:T(8,128)S(1)} %copy-done.2, f32[96,384]{1,0:T(8,128)S(1)} %copy-done.3), custom_call_target="tpu_custom_call" | custom-call | tf_op jit(solution)/shard_map/finish/pallas_call | solution.py:393
Async XLA Ops:
  74.8 1.0 %copy-start = (f32[32,3072]{1,0:T(8,128)S(1)}, f32[32,3072]{1,0:T(8,128)}, u32[]{:S(2)}) copy-start(f32[32,3072]{1,0:T(8,128)} %get-tuple-element.15.modes) | copy-start | bytes 1179652
  75.8 1.0 %copy-start.1 = (f32[32,3072]{1,0:T(8,128)S(1)}, f32[32,3072]{1,0:T(8,128)}, u32[]{:S(2)}) copy-start(f32[32,3072]{1,0:T(8,128)} %get-tuple-element.16.image) | copy-start | bytes 1179652
  76.7 0.9 %copy-start.2 = (f32[96,384]{1,0:T(8,128)S(1)}, f32[96,384]{1,0:T(8,128)}, u32[]{:S(2)}) copy-start(f32[96,384]{1,0:T(8,128)} %get-tuple-element.18.stiff) | copy-start | bytes 442372
  77.7 0.9 %copy-start.3 = (f32[96,384]{1,0:T(8,128)S(1)}, f32[96,384]{1,0:T(8,128)}, u32[]{:S(2)}) copy-start(f32[96,384]{1,0:T(8,128)} %get-tuple-element.19.mass) | copy-start | bytes 442372
  78.6 0.7 copy-start.4

commit v5 on v4

--- a/solution.py
+++ b/solution.py
@@ -21,6 +21,13 @@
 def product(a, b, dims=NN):
     mul = functools.partial(lax.dot_general, dimension_numbers=dims, preferred_element_type=jnp.float32)
     return mul(a[0], b[0]) + (mul(a[0], b[1]) + mul(a[1], b[0]))
+
+
+def stacked(a, b):
+    mul = functools.partial(jnp.dot, preferred_element_type=jnp.float32)
+    rows = a[0].shape[0]
+    both = mul(jnp.concatenate(a, axis=0), b[0])
+    return both[:rows] + (both[rows:] + mul(a[0], b[1]))
 
 
 def remote(src, dst, send, recv, device):
@@ -178,7 +185,7 @@
         def _(i):
             mine = search[i]
             picked = jnp.concatenate([mine, search[lax.rem(named[1, i], blk)]], axis=0)
-            image[i] = 4.0 * mine + product(split(values[i][:, :2 * block]), split(picked))
+            image[i] = 4.0 * mine + stacked(split(values[i][:, :2 * block]), split(picked))
 
         for k in range(2, nc, 2):
             arrival(on_col(-k), k, t).wait_recv()
@@ -215,7 +222,7 @@
                 for m, pair in enumerate(pieces):
                     i = 2 * (g * (per + 1) + m) + odd
                     picked = jnp.concatenate(pair, axis=0)
-                    image[i] += product(split(values[i][:, 2 * block:]), split(picked))
+                    image[i] += stacked(split(values[i][:, 2 * block:]), split(picked))
 
         img = split(image[t * bspan:(t + 1) * bspan].reshape(span, width))
         turned = product(rm, img, NT)
@@ -398,7 +405,7 @@
         ),
         in_specs=[vmem] * 5,
         out_specs=(vmem,) * 5,
-        compiler_params=pltpu.CompilerParams(vmem_limit_bytes=16 * 1024 * 1024),
+        compiler_params=pltpu.CompilerParams(vmem_limit_bytes=60 * 1024 * 1024),
         name="finish",
     )(*results)
     return modes_t.T, resid_t.T, theta, stiff.T, mass.T

time: 80.7 us -> 77.2 us (0.957)
  local copies, waits for them, and re-layouts: 5.8 us -> 1.28 us
  Pallas kernels: 73.9 us -> 75 us
    unnamed x10 -> x0, local copies, waits for them, and re-layouts: 4.52 us -> none
    pallas_call x1, Pallas kernels: 1.02 us -> 2.26 us  [shards(): pl.pallas_call(finish, out_shape=tuple((jax.ShapeDtypeStruct(shape, f32)...]
where the time goes in v5:
time: 77.2 us; the launch traced here: 77 us
  Pallas kernels  75 us (97%)
  local copies, waits for them, and re-layouts  1.28 us (2%)
    pallas_call x1, Pallas kernels, shards(): pl.pallas_call(functools.partial(kernel, nw, nc, parts, float(rows * nw))...  72.8 us
    pallas_call x1, Pallas kernels, shards(): pl.pallas_call(finish, out_shape=tuple((jax.ShapeDtypeStruct(shape, f32)...  2.26 us

profile of v5, /device:TPU:9, one launch (start us, length us, event | category | flops | bytes accessed | tf_op | source)
XLA Modules:
  0.0 77.0 jit_solution(15373381639702703982)
XLA Ops:
  0.6 1.3 %pad.4.named.wanted = s32[8,128]{1,0:T(8,128)} pad(s32[4,48]{1,0:T(4,128)} %bitcast.9, s32[]{:T(128)} %constant.0.clone.1), padding=0_4x0_80 | pad | bytes 4868 | tf_op jit(solution)/shard_map/jit(_pad)/pad | solution.py:353
  1.9 72.8 %step.1 = (f32[32,3072]{1,0:T(8,128)}, f32[32,3072]{1,0:T(8,128)}, f32[32,128]{1,0:T(8,128)}, f32[96,384]{1,0:T(8,128)}, f32[96,384]{1,0:T(8,128)}) custom-call(s32[8,128]{1,0:T(8,128)} %pad.4.named.wanted, s32[8,128]{1,0:T(8,128)} %pad.4.named.wanted, f32[96,3072]{1,0:T(8,128)} %bitcast.8, f32[48,64,256]{2,1,0:T(8,128)} %bitcast.7, f32[384,128]{1,0:T(8,128)} %ritz.1), custom_call_target="tpu_custom_call" | custom-call | tf_op jit(solution)/shard_map/step/pallas_call | solution.py:358
  74.7 2.3 %finish.1 = (f32[32,3072]{1,0:T(8,128)}, f32[32,3072]{1,0:T(8,128)}, f32[32]{0:T(128)}, f32[96,384]{1,0:T(8,128)}, f32[96,384]{1,0:T(8,128)}) custom-call(f32[32,3072]{1,0:T(8,128)} %get-tuple-element.15.modes, f32[32,3072]{1,0:T(8,128)} %get-tuple-element.16.image, f32[32,128]{1,0:T(8,128)} %get-tuple-element.17.theta, f32[96,384]{1,0:T(8,128)} %get-tuple-element.18.stiff, ...), custom_call_target="tpu_custom_call" | custom-call | tf_op jit(solution)/shard_map/finish/pallas_call | solution.py:400
